TPU v7x, 32 devices: a whole 2x2x4 slice. The times are simulated.
32 devices in a mesh: grp: 2 (over x), hist: 16 (over z, y, core).
Axes of the slice: x: 2, y: 2, z: 4, core: 2. Of those that a mesh axis runs over, the one named last changes fastest.
Arguments:
- item_ids: int32 [512], P(('grp', 'hist')), parts along dimension 0, may hold values from 0 to 16383
- item_table: bfloat16 [16384, 1024], P('hist'), may hold values from -6 to 6
- key_cache: bfloat16 [32768, 1024], P(('grp', 'hist')), parts along dimension 0, may hold values from -6 to 6
- value_cache: bfloat16 [32768, 1024], P(('grp', 'hist')), parts along dimension 0, may hold values from -6 to 6
- time_buckets: int32 [32768], P(('grp', 'hist')), parts along dimension 0, may hold values from 0 to 127
- window_start: int32 [2], P('grp'), parts along dimension 0, may hold values from 0 to 16384
- norm_gain: float32 [1024], replicated, may hold values from 0.25 to 1.75
- proj_in: bfloat16 [1024, 2048], replicated, may hold values from -0.1875 to 0.1875
- time_bias: float32 [16, 128], replicated, may hold values from -3 to 3
- pos_bias: float32 [16, 18], replicated, may hold values from -1 to 1
- out_gain: float32 [1024], replicated, may hold values from 0.25 to 1.75
- proj_out: bfloat16 [1024, 1024], replicated, may hold values from -0.1875 to 0.1875
Outputs:
- scored: bfloat16 [512, 1024], P(('grp', 'hist')), parts along dimension 0
There are 2 independent parts, one for each index of `grp`. A program takes and returns all parts, laid end to end along the dimension named above; an argument that names none is the same for every part. Nothing has to cross between parts.
All inputs are finite; a program needn't handle non-finite values.
Results may differ from a plain program's by a relative error of at most 0.0075.
Values may be sent and summed in bfloat16 or wider, within the bound.
A program may use at most 128 MiB of HBM per device.

v0:
```python
import functools

import jax
import jax.numpy as jnp
from jax import lax
from jax.experimental import pallas as pl
from jax.experimental.pallas import tpu as pltpu
from jax.sharding import PartitionSpec as P

LANES = 128
F32 = jnp.float32
BF16 = jnp.bfloat16


def silu(v):
    half = 0.5 * v
    return half + half * jnp.tanh(half)


def kernel(
    n,
    head_dim,
    group_pairs,
    ids_ref,
    table_hbm,
    key_hbm,
    value_hbm,
    tb_ref,
    start_ref,
    norm_gain_ref,
    win_hbm,
    time_bias_ref,
    pos_bias_ref,
    out_gain_ref,
    wout_hbm,
    o_ref,
    table_v,
    key_v,
    value_v,
    win_v,
    wout_v,
    idrow,
    idbuf,
    epart,
    ecore,
    esum,
    erx,
    efull,
    q,
    bias,
    p,
    prx,
    psum,
    arx,
    load_sem,
    id_s,
    id_r,
    ec_s,
    ec_r,
    ers_s,
    ers_r,
    eag_s,
    eag_r,
    fwd_s,
    fwd_r,
    p_s,
    p_r,
    a_s,
    a_r,
):
    me = lax.axis_index("hist")
    core = lax.rem(me, 2)
    other = 1 - core
    chip = me // 2
    nchip = n // 2
    partner = chip * 2 + other
    rows, width = table_v.shape
    events = key_v.shape[0]
    cpd = erx.shape[1]
    half_rows = nchip * cpd
    heads, ntb = time_bias_ref.shape
    npos = pos_bias_ref.shape[1]
    per = LANES // head_dim

    def remote(src, dst, ssem, rsem, dev):
        return pltpu.make_async_remote_copy(
            src_ref=src,
            dst_ref=dst,
            send_sem=ssem,
            recv_sem=rsem,
            device_id={"hist": dev},
            device_id_type=pl.DeviceIdType.MESH,
        )

    loads = [
        pltpu.make_async_copy(a, b, load_sem.at[i])
        for i, (a, b) in enumerate(
            (
                (table_hbm, table_v),
                (win_hbm, win_v),
                (key_hbm, key_v),
                (value_hbm, value_v),
                (wout_hbm, wout_v),
            )
        )
    ]
    for c in loads:
        c.start()

    idrow[...] = jnp.concatenate([ids_ref[...]] * (LANES // cpd), axis=1)
    barrier = pltpu.get_barrier_semaphore()

    def greet(d, _):
        pl.semaphore_signal(
            barrier,
            inc=1,
            device_id={"hist": lax.rem(me + d, n)},
            device_id_type=pl.DeviceIdType.MESH,
        )
        return 0

    lax.fori_loop(1, n, greet, 0)
    pl.semaphore_wait(barrier, n - 1)

    def send_ids(d, _):
        t = lax.rem(me + d, n)
        remote(idrow, idbuf.at[me], id_s, id_r, t).start()
        return 0

    lax.fori_loop(1, n, send_ids, 0)
    idbuf[me] = idrow[...]

    positions = me * events + lax.broadcasted_iota(jnp.int32, (1, events), 1)
    distance = 2 * events * n - start_ref[0] - positions
    buckets = tb_ref[...]
    onehot_t = jnp.where(
        buckets == lax.broadcasted_iota(jnp.int32, (ntb, events), 0), 1.0, 0.0
    ).astype(BF16)
    rest = time_bias_ref[...]
    time_part = jnp.zeros((heads, events), F32)
    for _ in range(3):
        head = rest.astype(BF16)
        rest = rest - head.astype(F32)
        time_part = time_part + jnp.dot(head, onehot_t, preferred_element_type=F32)
    far = jnp.broadcast_to(distance, (heads, events))
    pos_part = jnp.broadcast_to(pos_bias_ref[:, 0:1], (heads, events))
    for k in range(1, npos):
        pos_part = jnp.where(far >= 2**k, pos_bias_ref[:, k : k + 1], pos_part)
    bias[...] = (0.5 * (time_part + pos_part)).reshape(heads, 1, events)

    every = idbuf.at[pl.ds(0, n - 1)]
    ids_done = remote(every, every, id_s, id_r, partner)
    ids_done.wait_send()
    ids_done.wait_recv()
    loads[0].wait()

    per_vec = LANES // cpd
    nvec = half_rows // LANES
    lane = lax.broadcasted_iota(jnp.int32, (1, LANES), 1)
    table_first = me * rows

    def hot_rows(which):
        hots = []
        for v in range(nvec):
            row = jnp.zeros((1, LANES), jnp.int32)
            for j in range(per_vec):
                holder = (v * per_vec + j) * 2 + which
                row = jnp.where(lane // cpd == j, idbuf[holder], row)
            tall = jnp.transpose(jnp.broadcast_to(row, (LANES, LANES))) - table_first
            cols = lax.broadcasted_iota(jnp.int32, (LANES, LANES), 1)
            hots.append(
                jnp.concatenate(
                    [
                        jnp.where(tall == cols + k * LANES, 1.0, 0.0).astype(BF16)
                        for k in range(rows // LANES)
                    ],
                    axis=1,
                )
            )
        return hots

    nchunk = ec_s.shape[0]
    cwidth = width // nchunk
    chunks = [pl.ds(k * cwidth, cwidth) for k in range(nchunk)]

    def pick(which, hots, c):
        for v, hot in enumerate(hots):
            got = jnp.dot(hot, table_v[:, c], preferred_element_type=F32).astype(BF16)
            epart[which, pl.ds(v * per_vec, per_vec), :, c] = got.reshape(per_vec, cpd, cwidth)

    def to_partner(k):
        c = chunks[k]
        return remote(
            epart.at[other, :, :, c], ecore.at[:, :, c], ec_s.at[k], ec_r.at[k], partner
        )

    def owners(k):
        part = erx.at[pl.ds(0, nchip - 1), :, chunks[k]]
        return remote(part, part, ers_s.at[k], ers_r.at[k], partner)

    def gathered(k):
        part = efull.at[0, pl.ds(0, nchip - 1), :, chunks[k]]
        return remote(part, part, eag_s.at[k], eag_r.at[k], partner)

    def forward(k, which):
        half = efull.at[which, :, :, chunks[k]]
        return remote(half, half, fwd_s.at[k], fwd_r.at[k], partner)

    hots = hot_rows(other)
    for k in range(nchunk):
        pick(other, hots, chunks[k])
        to_partner(k).start()
    hots = hot_rows(core)
    for k in range(nchunk):
        pick(core, hots, chunks[k])
        to_partner(k).wait_recv()
        c = chunks[k]
        esum[:, :, c] = epart[core, :, :, c] + ecore[:, :, c]

        def send_e(d, _, k=k, c=c):
            t = lax.rem(chip + d, nchip)
            remote(
                esum.at[t, :, c], erx.at[chip, :, c], ers_s.at[k], ers_r.at[k], 2 * t + core
            ).start()
            return 0

        lax.fori_loop(1, nchip, send_e, 0)
        erx[chip, :, c] = esum[chip, :, c]

    home_parts = []
    for k in range(nchunk):
        owners(k).wait_recv()
        c = chunks[k]
        home_parts.append(jnp.sum(erx[:, :, c].astype(F32), axis=0))
        efull[core, chip, :, c] = home_parts[-1].astype(BF16)

        def send_g(d, _, k=k, c=c):
            t = lax.rem(chip + d, nchip)
            mine = efull.at[core, chip, :, c]
            remote(mine, mine, eag_s.at[k], eag_r.at[k], 2 * t + core).start()
            return 0

        lax.fori_loop(1, nchip, send_g, 0)
    home = jnp.concatenate(home_parts, axis=1)

    def normed_of(x):
        meansq = jnp.mean(x * x, axis=-1, keepdims=True)
        return (x * lax.rsqrt(meansq + 1e-6) * norm_gain_ref[...]).astype(BF16)

    loads[1].wait()
    gates = silu(
        jnp.dot(normed_of(home), win_v[:, width:], preferred_element_type=F32)
    ).astype(BF16)

    for k in range(nchunk):
        gathered(k).wait_recv()
        forward(k, core).start()

    def query(which):
        x = efull[which].reshape(half_rows, width).astype(F32)
        projected = jnp.dot(normed_of(x), win_v[:, :width], preferred_element_type=F32)
        scaled = silu(projected).astype(BF16) * jnp.asarray(0.5 * head_dim**-0.5, BF16)
        q[which] = scaled

    query(core)
    for k in range(nchunk):
        forward(k, other).wait_recv()
    query(other)
    loads[2].wait()
    loads[3].wait()

    groups = p_r.shape[0]
    gwidth = group_pairs * LANES
    lane_row = lax.broadcasted_iota(jnp.int32, (1, LANES), 1) // head_dim

    def gcols(g):
        return pl.ds(pl.multiple_of(g * gwidth, gwidth), gwidth)

    def share(g):
        c = gcols(g)
        return remote(p.at[other, :, :, c], prx.at[:, :, c], p_s, p_r.at[g], partner)

    def finish(g):
        share(g).wait_recv()
        c = gcols(g)
        psum[:, :, c] = (p[core, :, :, c].astype(F32) + prx[:, :, c].astype(F32)).astype(BF16)

        def send_a(d, _):
            t = lax.rem(chip + d, nchip)
            remote(
                psum.at[t, :, c], arx.at[chip, :, c], a_s, a_r, 2 * t + core
            ).start()
            return 0

        lax.fori_loop(1, nchip, send_a, 0)
        arx[chip, :, c] = psum[chip, :, c]

    def attend(g, _):
        for u in range(group_pairs):
            pair = g * group_pairs + u
            c = pl.ds(pl.multiple_of(pair * LANES, LANES), LANES)
            qp = q[:, :, c].reshape(2 * half_rows, LANES)
            kp = key_v[:, c]
            vp = value_v[:, c]
            out = None
            for h in range(per):
                qm = jnp.where(lane_row == h, qp, jnp.zeros_like(qp))
                s = lax.dot_general(
                    qm, kp, (((1,), (1,)), ((), ())), preferred_element_type=F32
                )
                half = s + bias[pair * per + h]
                w = (half + half * jnp.tanh(half)).astype(BF16)
                o = jnp.dot(w, vp, preferred_element_type=F32)
                out = o if out is None else jnp.where(lane_row == h, o, out)
            p[:, :, :, c] = out.astype(BF16).reshape(2, nchip, cpd, LANES)
        share(g).start()

        @pl.when(g >= 1)
        def _():
            finish(g - 1)

        return 0

    lax.fori_loop(0, groups, attend, 0)
    finish(groups - 1)
    loads[4].wait()

    whole = arx.at[pl.ds(0, nchip - 1)]
    sums = remote(whole, whole, a_s, a_r, partner)
    sums.wait_recv()

    attended = jnp.sum(arx[...].astype(F32), axis=0)
    centred = attended - jnp.mean(attended, axis=-1, keepdims=True)
    variance = jnp.mean(centred * centred, axis=-1, keepdims=True)
    gated = (
        centred * lax.rsqrt(variance + 1e-5) * out_gain_ref[...] * gates.astype(F32)
    ).astype(BF16)
    o_ref[...] = (home + jnp.dot(gated, wout_v[...], preferred_element_type=F32)).astype(BF16)

    for k in range(nchunk):
        to_partner(k).wait_send()
        owners(k).wait_send()
        gathered(k).wait_send()
        forward(k, core).wait_send()
    remote(prx, prx, p_s, p_r.at[0], partner).wait_send()
    sums.wait_send()


def on_device(
    n,
    item_ids,
    item_table,
    key_cache,
    value_cache,
    time_buckets,
    window_start,
    norm_gain,
    proj_in,
    time_bias,
    pos_bias,
    out_gain,
    proj_out,
):
    cpd = item_ids.shape[0]
    rows, width = item_table.shape
    events = key_cache.shape[0]
    heads = time_bias.shape[0]
    nchip = n // 2
    half_rows = nchip * cpd
    group_pairs = 2
    nchunk = 2
    groups = width // (group_pairs * LANES)
    dma = pltpu.SemaphoreType.DMA
    vmem = pl.BlockSpec(memory_space=pltpu.VMEM)
    smem = pl.BlockSpec(memory_space=pltpu.SMEM)
    hbm = pl.BlockSpec(memory_space=pl.ANY)
    return pl.pallas_call(
        functools.partial(kernel, n, width // heads, group_pairs),
        out_shape=jax.ShapeDtypeStruct((cpd, width), BF16),
        in_specs=[vmem, hbm, hbm, hbm, vmem, smem, vmem, hbm, vmem, vmem, vmem, hbm],
        out_specs=vmem,
        scratch_shapes=[
            pltpu.VMEM((rows, width), BF16),
            pltpu.VMEM((events, width), BF16),
            pltpu.VMEM((events, width), BF16),
            pltpu.VMEM(proj_in.shape, BF16),
            pltpu.VMEM(proj_out.shape, BF16),
            pltpu.VMEM((1, LANES), jnp.int32),
            pltpu.VMEM((n, 1, LANES), jnp.int32),
            pltpu.VMEM((2, nchip, cpd, width), BF16),
            pltpu.VMEM((nchip, cpd, width), BF16),
            pltpu.VMEM((nchip, cpd, width), BF16),
            pltpu.VMEM((nchip, cpd, width), BF16),
            pltpu.VMEM((2, nchip, cpd, width), BF16),
            pltpu.VMEM((2, half_rows, width), BF16),
            pltpu.VMEM((heads, 1, events), F32),
            pltpu.VMEM((2, nchip, cpd, width), BF16),
            pltpu.VMEM((nchip, cpd, width), BF16),
            pltpu.VMEM((nchip, cpd, width), BF16),
            pltpu.VMEM((nchip, cpd, width), BF16),
            dma((5,)),
            dma,
            dma,
            dma((nchunk,)),
            dma((nchunk,)),
            dma((nchunk,)),
            dma((nchunk,)),
            dma((nchunk,)),
            dma((nchunk,)),
            dma((nchunk,)),
            dma((nchunk,)),
            dma,
            dma((groups,)),
            dma,
            dma,
        ],
        compiler_params=pltpu.CompilerParams(
            collective_id=0, has_side_effects=True, vmem_limit_bytes=56 * 1024 * 1024
        ),
    )(
        item_ids[None, :],
        item_table,
        key_cache,
        value_cache,
        time_buckets[None, :],
        window_start,
        norm_gain[None, :],
        proj_in,
        time_bias,
        pos_bias,
        out_gain[None, :],
        proj_out,
    )


def solution(mesh):
    placed = (
        P(("grp", "hist")),
        P("hist", None),
        P(("grp", "hist"), None),
        P(("grp", "hist"), None),
        P(("grp", "hist")),
        P("grp"),
        P(),
        P(),
        P(),
        P(),
        P(),
        P(),
    )
    return jax.shard_map(
        functools.partial(on_device, mesh.shape["hist"]),
        mesh=mesh,
        in_specs=placed,
        out_specs=P(("grp", "hist"), None),
        check_vma=False,
    )
```

profile of v0, /device:TPU:0, one launch (start us, length us, event | category | flops | bytes accessed | tf_op | source)
XLA Modules:
  0.0 41.8 jit_solution(12208862387496837043)
XLA Ops:
  0.7 39.7 %shard_map.118 = bf16[16,1024]{1,0:T(8,128)(2,1)} custom-call(s32[1,16]{1,0:T(1,128)} %bitcast.7, bf16[1024,1024]{1,0:T(8,128)(2,1)} %table_hbm.1, bf16[1024,1024]{1,0:T(8,128)(2,1)} %key_hbm.1, bf16[1024,1024]{1,0:T(8,128)(2,1)} %value_hbm.1, s32[1,1024]{1,0:T(1,128)} %bitcast.4, s32[1]{0:T(128)S(6)} %copy.14.start_ref, f32[1,1024]{1,0:T(1,128)} %bitcast.5, ...), custom_call_target="tpu_custom_call" | custom-call | tf_op jit(solution)/shard_map/pallas_call | solution.py:377
  40.4 1.4 %copy.15 = bf16[16,1024]{1,0:T(8,128)(2,1)} copy(bf16[16,1024]{1,0:T(8,128)(2,1)} %shard_map.118) | data formatting | bytes 65536
where the time goes:
time: 42 us; the launch traced here: 41.8 us
  Pallas kernels  39.7 us (95%)
  local copies, waits for them, and re-layouts  1.38 us (3%)
  between operations  0.66 us (2%)
    pallas_call x1, Pallas kernels, on_device(): pl.pallas_call(functools.partial(kernel, n, width // heads, group_pairs),...  39.7 us
    unnamed x1, local copies, waits for them, and re-layouts  1.38 us

commit v1 on v0

--- a/solution.py
+++ b/solution.py
@@ -120,16 +120,6 @@
         return 0
 
     lax.fori_loop(1, n, greet, 0)
-    pl.semaphore_wait(barrier, n - 1)
-
-    def send_ids(d, _):
-        t = lax.rem(me + d, n)
-        remote(idrow, idbuf.at[me], id_s, id_r, t).start()
-        return 0
-
-    lax.fori_loop(1, n, send_ids, 0)
-    idbuf[me] = idrow[...]
-
     positions = me * events + lax.broadcasted_iota(jnp.int32, (1, events), 1)
     distance = 2 * events * n - start_ref[0] - positions
     buckets = tb_ref[...]
@@ -147,6 +137,16 @@
     for k in range(1, npos):
         pos_part = jnp.where(far >= 2**k, pos_bias_ref[:, k : k + 1], pos_part)
     bias[...] = (0.5 * (time_part + pos_part)).reshape(heads, 1, events)
+
+    pl.semaphore_wait(barrier, n - 1)
+
+    def send_ids(d, _):
+        t = lax.rem(me + d, n)
+        remote(idrow, idbuf.at[me], id_s, id_r, t).start()
+        return 0
+
+    lax.fori_loop(1, n, send_ids, 0)
+    idbuf[me] = idrow[...]
 
     every = idbuf.at[pl.ds(0, n - 1)]
     ids_done = remote(every, every, id_s, id_r, partner)
@@ -335,7 +335,7 @@
     gated = (
         centred * lax.rsqrt(variance + 1e-5) * out_gain_ref[...] * gates.astype(F32)
     ).astype(BF16)
-    o_ref[...] = (home + jnp.dot(gated, wout_v[...], preferred_element_type=F32)).astype(BF16)
+    o_ref[...] = home + jnp.dot(gated, wout_v[...], preferred_element_type=F32)
 
     for k in range(nchunk):
         to_partner(k).wait_send()
@@ -376,7 +376,7 @@
     hbm = pl.BlockSpec(memory_space=pl.ANY)
     return pl.pallas_call(
         functools.partial(kernel, n, width // heads, group_pairs),
-        out_shape=jax.ShapeDtypeStruct((cpd, width), BF16),
+        out_shape=jax.ShapeDtypeStruct((cpd, width), F32),
         in_specs=[vmem, hbm, hbm, hbm, vmem, smem, vmem, hbm, vmem, vmem, vmem, hbm],
         out_specs=vmem,
         scratch_shapes=[
@@ -430,7 +430,7 @@
         pos_bias,
         out_gain[None, :],
         proj_out,
-    )
+    ).astype(BF16)
 
 
 def solution(mesh):

time: 42 us -> 42.1 us (level)
  other arithmetic: 0 us -> 1.46 us
  local copies, waits for them, and re-layouts: 1.38 us -> 0 us
    convert_element_type x0 -> x1, other arithmetic: none -> 1.46 us  [on_device(): return pl.pallas_call(functools.partial(kernel, n, width // heads, group_...]
    unnamed x1 -> x0, local copies, waits for them, and re-layouts: 1.38 us -> none
where the time goes in v1:
time: 42.1 us; the launch traced here: 41.9 us
  Pallas kernels  39.7 us (94%)
  other arithmetic  1.46 us (3%)
  between operations  0.66 us (2%)
    pallas_call x1, Pallas kernels, on_device(): pl.pallas_call(functools.partial(kernel, n, width // heads, group_pairs),...  39.7 us
    convert_element_type x1, other arithmetic, on_device(): return pl.pallas_call(functools.partial(kernel, n, width // heads, group_...  1.46 us

profile of v1, /device:TPU:0, one launch (start us, length us, event | category | flops | bytes accessed | tf_op | source)
XLA Modules:
  0.0 41.9 jit_solution(7114444260829677980)
XLA Ops:
  0.7 39.7 %shard_map.118 = f32[16,1024]{1,0:T(8,128)} custom-call(s32[1,16]{1,0:T(1,128)} %bitcast.7, bf16[1024,1024]{1,0:T(8,128)(2,1)} %table_hbm.1, bf16[1024,1024]{1,0:T(8,128)(2,1)} %key_hbm.1, bf16[1024,1024]{1,0:T(8,128)(2,1)} %value_hbm.1, s32[1,1024]{1,0:T(1,128)} %bitcast.4, s32[1]{0:T(128)S(6)} %copy.13.start_ref, f32[1,1024]{1,0:T(1,128)} %bitcast.5, ...), custom_call_target="tpu_custom_call" | custom-call | tf_op jit(solution)/shard_map/pallas_call | solution.py:377
  40.4 1.5 %convert_element_type.3 = bf16[16,1024]{1,0:T(8,128)(2,1)} convert(f32[16,1024]{1,0:T(8,128)} %shard_map.118) | non-fusion elementwise | flops 16384 | bytes 98304 | tf_op jit(solution)/shard_map/convert_element_type | solution.py:433
